TPU v7x, 32 devices: a whole 2x2x4 slice. The times are simulated.
32 devices in a mesh: dp: 4 (over y, x), ctx: 4 (over z), mp: 2 (over core).
Axes of the slice: x: 2, y: 2, z: 4, core: 2. Of those that a mesh axis runs over, the one named last changes fastest.
Arguments:
- tokens: bfloat16 [4, 512, 4096], P('dp', 'ctx'), may hold values from -52 to 52
- x_weight: bfloat16 [4096, 8192], P(('dp', 'ctx'), 'mp'), may hold values from -0.09375 to 0.09375
- bc_weight: bfloat16 [4096, 1024], P(('dp', 'ctx'), 'mp'), may hold values from -0.09375 to 0.09375
- dt_weight: bfloat16 [4096, 128], P(('dp', 'ctx'), 'mp'), may hold values from -0.0234375 to 0.0234375
- conv_x: float32 [5, 8192], P(None, 'mp'), may hold values from -0.5 to 0.5
- conv_bc: float32 [5, 1024], P(None, 'mp'), may hold values from -0.5 to 0.5
- dt_bias: float32 [128], P('mp'), may hold values from -4.5 to -2.5
- a_log: float32 [128], P('mp')
- d_skip: float32 [128], P('mp'), may hold values from 0.5 to 1.5
- norm_gain: float32 [8192], P('mp'), may hold values from 0.5 to 1.5
Outputs:
- mixer_out: bfloat16 [4, 512, 8192], P('dp', 'ctx', 'mp')
- kurtosis: float32 [4096], P('mp')
All inputs are finite; a program needn't handle non-finite values.
Results may differ from a plain program's by a relative error of at most 0.015.
Values may be sent and summed in bfloat16 or wider, within the bound.
A program may use at most 128 MiB of HBM per device.

v0:
```python
import jax
import jax.numpy as jnp
from jax import lax
from jax.sharding import PartitionSpec as P

ROOT = 64
HEADS = 128
G = 4
NS = 128


HIGH = lax.Precision.HIGHEST


def passed_along(value, axis, steps):
    count = lax.axis_size(axis)
    first, last = (max(0, -steps), min(count, count - steps))
    return lax.ppermute(value, axis, [(source, source + steps) for source in range(first, last)])


def entering(array, axis, combine, identity):
    length, place = (lax.axis_size(axis), lax.axis_index(axis))
    everything = jax.tree.map(
        lambda part, kind: lax.all_gather(part.astype(kind), axis),
        array,
        (jnp.bfloat16, jnp.bfloat16),
    )
    start = jax.tree.map(
        lambda part, zero: jnp.broadcast_to(jnp.asarray(zero, part.dtype), part.shape),
        array,
        identity,
    )

    def step(k, before):
        reached = k < place
        new = combine(
            before, jax.tree.map(lambda part, own: part[k].astype(own.dtype), everything, array)
        )
        return jax.tree.map(lambda a, b: jnp.where(reached, a, b), new, before)

    return lax.fori_loop(0, length, step, start)


def hadamard_signs(sign_order):
    row_index = lax.broadcasted_iota(jnp.int32, (sign_order, sign_order), 0)
    col_index = lax.broadcasted_iota(jnp.int32, (sign_order, sign_order), 1)
    common = jnp.bitwise_and(row_index, col_index)
    parity = jnp.zeros((sign_order, sign_order), jnp.int32)
    for bit_index in range(sign_order.bit_length() - 1):
        parity = parity + jnp.bitwise_and(jnp.right_shift(common, bit_index), 1)
    return 1.0 - 2.0 * jnp.bitwise_and(parity, 1).astype(jnp.float32)


def kurtosis_from(powers, row_count):
    average = powers[0] / row_count
    second = powers[1] / row_count - average * average
    fourth = (
        powers[3] / row_count
        - 4.0 * average * powers[2] / row_count
        + 6.0 * average * average * powers[1] / row_count
        - 3.0 * average * average * average * average
    )
    return fourth / (second * second + 1e-06)


def chain_states(earlier, later):
    return (earlier[0] * later[0], later[0][:, :, None, None] * earlier[1] + later[1])


def shards(
    tokens, x_weight, bc_weight, dt_weight, conv_x, conv_bc, dt_bias, a_log, d_skip, norm_gain
):
    tok_rows = tokens.shape[1]
    model_width = tokens.shape[2]
    signs = hadamard_signs(ROOT)
    blocks = tokens.reshape(tok_rows, ROOT, ROOT)
    first_pass = jnp.einsum(
        "tab,ac->tcb", blocks, signs.astype(jnp.bfloat16), preferred_element_type=jnp.float32
    )
    second = jnp.einsum("tcb,bd->tcd", first_pass, signs, precision=HIGH)
    rotated = (second.reshape(tok_rows, model_width) / ROOT).astype(jnp.bfloat16)
    channel_share = model_width // lax.axis_size("mp")
    own_cols = lax.dynamic_slice_in_dim(
        rotated, lax.axis_index("mp") * channel_share, channel_share, 1
    ).astype(jnp.float32)
    square = own_cols * own_cols
    powers = jnp.stack(
        [
            jnp.sum(own_cols, 0),
            jnp.sum(square, 0),
            jnp.sum(square * own_cols, 0),
            jnp.sum(square * square, 0),
        ]
    )
    row_count = float(tok_rows * lax.axis_size("dp") * lax.axis_size("ctx"))
    totals = lax.psum(powers, ("dp", "ctx"))
    kurtosis = kurtosis_from(totals, row_count)
    panels = (
        lax.all_gather(x_weight, ("dp", "ctx"), axis=0, tiled=True),
        lax.all_gather(bc_weight, ("dp", "ctx"), axis=0, tiled=True),
        lax.all_gather(dt_weight, ("dp", "ctx"), axis=0, tiled=True),
    )
    projected = tuple(
        (jnp.dot(rotated, panel, preferred_element_type=jnp.float32) for panel in panels)
    )
    x_cols = x_weight.shape[1]
    joined = jnp.concatenate(
        [projected[0].astype(jnp.bfloat16), projected[1].astype(jnp.bfloat16)], 1
    )
    dt_proj = lax.optimization_barrier(projected[2].astype(jnp.bfloat16))
    conv_taps = jnp.concatenate([conv_x, conv_bc], 1)
    kernel = conv_taps.shape[0] - 1
    rim_rows = passed_along(joined[tok_rows - (kernel - 1) :], "ctx", 1)
    padded = jnp.concatenate([rim_rows, joined], 0)
    conv_sum = conv_taps[kernel]
    for tap_index in range(kernel):
        conv_sum = conv_sum + conv_taps[tap_index] * padded[tap_index : tap_index + tok_rows]
    convolved = jax.nn.silu(conv_sum).astype(jnp.bfloat16)
    x_conv = convolved[:, :x_cols]
    group_all = lax.all_gather(convolved[:, x_cols:], "mp", axis=1, tiled=True)
    heads_dev = dt_weight.shape[1]
    head_size = x_cols // heads_dev
    per_group = HEADS // G
    groups_here = max(1, heads_dev // per_group)
    heads_local = heads_dev // groups_here
    first_group = lax.axis_index("mp") * heads_dev // per_group
    write_all = group_all[:, : G * NS].reshape(tok_rows, G, NS)
    read_all = group_all[:, G * NS :].reshape(tok_rows, G, NS)
    write_here = lax.dynamic_slice_in_dim(write_all, first_group, groups_here, 1)
    read_here = lax.dynamic_slice_in_dim(read_all, first_group, groups_here, 1)
    step_size = jax.nn.softplus(dt_proj.astype(jnp.float32) + dt_bias)
    decay_rate = step_size * jnp.exp(a_log)
    cumulative = jnp.cumsum(decay_rate, 0)
    block_end = cumulative[-1]
    causal = lax.broadcasted_iota(jnp.int32, (tok_rows, tok_rows), 0) >= lax.broadcasted_iota(
        jnp.int32, (tok_rows, tok_rows), 1
    )
    spread = cumulative.T[:, :, None] - cumulative.T[:, None, :]
    decay_mask = jnp.where(causal, jnp.exp(-jnp.where(causal, spread, 0.0)), 0.0)
    scores = jnp.einsum("tgn,sgn->gts", read_here, write_here, preferred_element_type=jnp.float32)
    weights = (
        scores[:, None]
        * decay_mask.reshape(groups_here, heads_local, tok_rows, tok_rows)
        * step_size.T.reshape(groups_here, heads_local, 1, tok_rows)
    ).astype(jnp.bfloat16)
    x_heads = x_conv.reshape(tok_rows, groups_here, heads_local, head_size)
    within_block = jnp.einsum(
        "ghts,sghp->tghp", weights, x_heads, preferred_element_type=jnp.float32
    )
    update = (
        (jnp.exp(-(block_end - cumulative)) * step_size).reshape(
            tok_rows, groups_here, heads_local
        )[..., None]
        * x_heads
    ).astype(jnp.bfloat16)
    contrib = jnp.einsum("sghp,sgn->ghpn", update, write_here, preferred_element_type=jnp.float32)
    identity = (jnp.ones((groups_here, heads_local), jnp.float32), jnp.zeros_like(contrib))
    carried = entering(
        (jnp.exp(-block_end).reshape(groups_here, heads_local), contrib),
        "ctx",
        chain_states,
        identity,
    )
    from_before = jnp.exp(-cumulative).reshape(tok_rows, groups_here, heads_local)[
        ..., None
    ] * jnp.einsum("tgn,ghpn->tghp", read_here.astype(jnp.float32), carried[1], precision=HIGH)
    output_raw = (
        within_block
        + from_before
        + d_skip.reshape(groups_here, heads_local)[None, :, :, None] * x_heads.astype(jnp.float32)
    )
    mean_square = jnp.mean(output_raw * output_raw, -1, keepdims=True)
    normed = (
        output_raw
        * lax.rsqrt(mean_square + 1e-05)
        * norm_gain.reshape(groups_here, heads_local, head_size)
    )
    return (normed.reshape(1, tok_rows, x_cols).astype(jnp.bfloat16), kurtosis)


def solution(mesh):
    return jax.shard_map(
        shards,
        mesh=mesh,
        in_specs=(
            P("dp", "ctx", None),
            P(("dp", "ctx"), "mp"),
            P(("dp", "ctx"), "mp"),
            P(("dp", "ctx"), "mp"),
            P(None, "mp"),
            P(None, "mp"),
            P("mp"),
            P("mp"),
            P("mp"),
            P("mp"),
        ),
        out_specs=(P("dp", "ctx", "mp"), P("mp")),
        check_vma=False,
    )
```

profile of v0, /device:TPU:0, one launch (start us, length us, event | category | flops | bytes accessed | tf_op | source)
XLA Modules:
  0.0 582.4 jit_solution(14779792656535856881)
XLA Ops:
  9.4 49.2 %all_gather.25 = bf16[4096,64]{0,1:T(8,128)(2,1)S(1)} all-gather(bf16[256,64]{0,1:T(8,128)(2,1)S(1)} %copy-done.4), channel_id=1, replica_groups=mesh['dp'=4,'ctx'=4,'mp'=2] {'dp','ctx'}, dimensions={0}, use_global_device_ids=true | all-gather | bytes 557056 | tf_op jit(solution)/shard_map/all_gather | solution.py:101
  58.6 0.9 convolution_bitcast_fusion
  59.6 3.3 multiply_convert_fusion.4
  64.5 27.2 %all-gather.7.cloned.1.call-done = bf16[4096,512]{1,0:T(8,128)(2,1)} async-done(((bf16[256,512]{1,0:T(8,128)(2,1)}), bf16[4096,512]{1,0:T(8,128)(2,1)}) %all-gather.7.cloned.1.call-update) | async-done | bytes 4194320 | tf_op jit(solution)/shard_map/all_gather | solution.py:100
  91.7 2.9 convolution_convert_fusion.2
  94.6 349.4 %all-gather.5.cloned.1.call-done = bf16[4096,4096]{1,0:T(8,128)(2,1)} async-done(((bf16[256,4096]{1,0:T(8,128)(2,1)}), bf16[4096,4096]{1,0:T(8,128)(2,1)}) %all-gather.5.cloned.1.call-update) | async-done | bytes 33554448 | tf_op jit(solution)/shard_map/all_gather | solution.py:99
  444.0 13.1 %convolution_convert_fusion = bf16[128,4096]{1,0:T(8,128)(2,1)S(1)} fusion(bf16[128,4096]{0,1:T(8,128)(2,1)S(1)} %bitcast.71, bf16[4096,4096]{1,0:T(8,128)(2,1)} %all-gather.5.cloned.1.call-done), kind=kOutput, calls=%fused_computation.3 | convolution fusion | flops 4295491584 | bytes 35651584 | tf_op jit(solution)/shard_map/dot_general | solution.py:104
  457.1 1.5 collective-permute-start
  458.9 1.3 collective-permute-done
  460.6 1.8 multiply_convert_fusion.1
  462.5 2.0 all_gather.24
  465.4 2.3 convolution_convert_fusion.1
  469.1 1.3 mul.246
  470.5 12.0 %all_gather.26 = bf16[4,2,32]{2,1,0:T(2,128)(2,1)S(1)} all-gather(bf16[1,2,32]{2,1,0:T(2,128)(2,1)} %convert_element_type.124), channel_id=1, replica_groups=mesh['dp'=4,'ctx'=4,'mp'=2] {'ctx'}, dimensions={0}, use_global_device_ids=true | all-gather | bytes 640 | tf_op jit(solution)/shard_map/all_gather | solution.py:24
  482.5 1.0 convert_reduce_fusion
  483.6 74.8 %psum.7 = f32[4,2048]{1,0:T(4,128)S(1)} all-reduce(f32[4,2048]{1,0:T(4,128)S(1)} %pad_maximum_fusion.1), channel_id=1, replica_groups=mesh['dp'=4,'ctx'=4,'mp'=2] {'dp','ctx'}, use_global_device_ids=true, to_apply=%region_8.9 | all-reduce | flops 8192 | bytes 65536 | tf_op jit(solution)/shard_map/psum | solution.py:96
  559.3 3.9 fusion.1
  563.3 7.3 %while.14 = (s32[]{:T(128)}, f32[2,32,64,128]{3,2,1,0:T(8,128)S(1)}, s32[]{:T(128)}, bf16[4,2,32]{2,1,0:T(2,128)(2,1)S(1)}, bf16[4,2,32,64,128]{4,3,2,1,0:T(8,128)(2,1)}, /*index=5*/s32[]{:T(128)}, s32[]{:T(128)}) while((s32[]{:T(128)}, f32[2,32,64,128]{3,2,1,0:T(8,128)S(1)}, s32[]{:T(128)}, bf16[4,2,32]{2,1,0:T(2,128)(2,1)S(1)}, ...), condition=%wide.region_2.0_spmd.clone, body=%wide.region_1.0_spmd.clone.sunk | while | flops 2621508 | bytes 5243625 | solution.py:41
  563.3 1.8 fusion.64
  565.2 1.8 fusion.64
  567.0 1.8 fusion.64
  568.8 1.8 fusion.64
  570.6 3.2 multiply_reduce_fusion
  574.6 1.3 copy.41
  (69 shorter events, 8.4 us)
Async XLA Ops:
  7.2 1.6 copy-start.2
  7.2 84.5 %all-gather.7.cloned.1.call-start = ((), (), s32[]{:S(2)}) async-start(), calls=%async_computation.1 | async-start | bytes 4456448 | tf_op jit(solution)/shard_map/all_gather | solution.py:100
  7.9 1.5 copy-start.4
  7.9 436.1 %all-gather.5.cloned.1.call-start = ((), (), s32[]{:S(2)}) async-start(), calls=%async_computation | async-start | bytes 35651584 | tf_op jit(solution)/shard_map/all_gather | solution.py:99
  8.7 554.6 %all-gather.9.cloned.1.call-start = ((), (), s32[]{:S(2)}) async-start(), calls=%async_computation.2 | async-start | bytes 5242880 | tf_op jit(solution)/shard_map/all_gather | solution.py:24
  59.5 3.7 copy-start.10
  59.5 3.7 copy-start.8
  59.5 4.2 copy-start.3
  59.6 4.2 copy-start.7
  457.1 3.2 collective-permute-start
  465.3 2.4 copy-start
  465.3 5.2 copy-start.6
  465.4 94.0 %copy-start.5 = (f32[128,64]{0,1:T(8,128)S(1)}, f32[128,64]{0,1:T(8,128)}, u32[]{:S(2)}) copy-start(f32[128,64]{0,1:T(8,128)} %get-tuple-element.148) | copy-start | bytes 98308
  563.3 7.3 %copy-start.1 = (bf16[128,4096]{0,1:T(8,128)(2,1)S(1)}, bf16[128,4096]{0,1:T(8,128)(2,1)}, u32[]{:S(2)}) copy-start(bf16[128,4096]{0,1:T(8,128)(2,1)} %copy-done) | copy-start | bytes 3145732
  563.3 7.3 %copy-start.9 = (f32[2,32]{1,0:T(2,128)S(1)}, f32[2,32]{1,0:T(2,128)}, u32[]{:S(2)}) copy-start(f32[2,32]{1,0:T(2,128)} %mul.246) | copy-start | bytes 772
Sparse Core Ops, SparseCore 0:
  10.8 80.8 all-gather.6
  94.5 349.4 all-gather.4
  467.8 83.7 all-gather.8
where the time goes:
time: 583 us; the launch traced here: 582 us
  waiting for transfers between devices  379 us (65%)
  blocking collectives  138 us (24%)
  matrix products  30.1 us (5%)
  between operations  14.2 us (2%)
  other arithmetic  12.9 us (2%)
  local copies, waits for them, and re-layouts  6.22 us (1%)
    all_gather x1, waiting for transfers between devices, shards(): lax.all_gather(x_weight, ('dp', 'ctx'), axis=0, tiled=True)  349 us
    psum x1, blocking collectives, shards(): totals = lax.psum(powers, ('dp', 'ctx'))  74.8 us
    all_gather x1, blocking collectives, shards(): lax.all_gather(dt_weight, ('dp', 'ctx'), axis=0, tiled=True)  49.2 us
    all_gather x1, waiting for transfers between devices, shards(): lax.all_gather(bc_weight, ('dp', 'ctx'), axis=0, tiled=True)  27.2 us
    dot_general x3, matrix products, shards(): jnp.dot(rotated, panel, preferred_element_type=jnp.float32)  16.3 us
    all_gather x1, blocking collectives, entering(): lax.all_gather(part.astype(kind), axis)  12 us
  transfers between devices with their start and end apart: 4, of which 3 were waited for; matrix products, arithmetic and copies ran while one was open for 3% of the time, Pallas kernels for 0%

commit v1 on v0

--- a/solution.py
+++ b/solution.py
@@ -67,7 +67,7 @@
     return (earlier[0] * later[0], later[0][:, :, None, None] * earlier[1] + later[1])
 
 
-def shards(
+def shards_by_rows(
     tokens, x_weight, bc_weight, dt_weight, conv_x, conv_bc, dt_bias, a_log, d_skip, norm_gain
 ):
     tok_rows = tokens.shape[1]
@@ -178,6 +178,171 @@
     return (normed.reshape(1, tok_rows, x_cols).astype(jnp.bfloat16), kurtosis)
 
 
+def hadamard(order):
+    return hadamard_signs(order)
+
+
+def rotated_half(tokens, which):
+    rows, width = tokens.shape
+    lanes = 256
+    tiles = width // lanes
+    first = jnp.einsum(
+        "tab,bd->tad",
+        tokens.reshape(rows, tiles, lanes),
+        hadamard(lanes).astype(jnp.bfloat16),
+        preferred_element_type=jnp.float32,
+    )
+    sign = 1.0 - 2.0 * which.astype(jnp.float32)
+    kept = first[:, : tiles // 2] + sign * first[:, tiles // 2 :]
+    span = tiles // 4
+    while span:
+        pairs = kept.reshape(rows, tiles // 4 // span, 2, span, lanes)
+        kept = jnp.stack([pairs[:, :, 0] + pairs[:, :, 1], pairs[:, :, 0] - pairs[:, :, 1]], 2)
+        span //= 2
+    return (kept.reshape(rows, width // 2) / (width**0.5)).astype(jnp.bfloat16)
+
+
+def swapped(value):
+    return lax.ppermute(value, "mp", [(0, 1), (1, 0)])
+
+
+def own_bc(array, me):
+    half = array.shape[1] // 2
+    keep = lax.dynamic_slice_in_dim(array, me * half, half, 1)
+    give = lax.dynamic_slice_in_dim(array, (1 - me) * half, half, 1)
+    got = swapped(give)
+    return jnp.where(me == 0, keep, got), jnp.where(me == 0, got, keep)
+
+
+def own_cut(array, place, count, axis):
+    size = array.shape[axis] // count
+    return lax.dynamic_slice_in_dim(array, place * size, size, axis)
+
+
+ROWS = ("dp", "ctx")
+
+
+def shards_by_heads(
+    tokens, x_weight, bc_weight, dt_weight, conv_x, conv_bc, dt_bias, a_log, d_skip, norm_gain
+):
+    me = lax.axis_index("mp")
+    place = lax.axis_index(ROWS)
+    count = lax.axis_size(ROWS)
+    seqs, blks = lax.axis_size("dp"), lax.axis_size("ctx")
+    tok_rows, width = tokens.shape[1:]
+    all_rows = count * tok_rows
+    depth = x_weight.shape[0]
+    heads = dt_weight.shape[1] // count
+    groups_here = dt_weight.shape[1] // (HEADS // G)
+    per_group = count // groups_here
+    bc_cols = groups_here * NS // count
+    x_cols = x_weight.shape[1] // count
+    head_size = x_cols // heads
+
+    write_w, read_w = own_bc(bc_weight, me)
+    pieces = jnp.concatenate(
+        [
+            x_weight.reshape(depth, count, x_cols),
+            write_w.reshape(depth, count, bc_cols),
+            read_w.reshape(depth, count, bc_cols),
+            dt_weight.reshape(depth, count, heads),
+        ],
+        2,
+    )
+    panel = lax.all_to_all(pieces, ROWS, 1, 0, tiled=True).reshape(width, -1)
+    half = width // 2
+    panel_keep = lax.dynamic_slice_in_dim(panel, me * half, half, 0)
+    panel_got = swapped(lax.dynamic_slice_in_dim(panel, (1 - me) * half, half, 0))
+
+    rotated = lax.all_gather(rotated_half(tokens[0], me), ROWS, axis=0, tiled=True)
+    wide = rotated.astype(jnp.float32)
+    square = wide * wide
+    powers = [
+        jnp.sum(wide, 0),
+        jnp.sum(square, 0),
+        jnp.sum(square * wide, 0),
+        jnp.sum(square * square, 0),
+    ]
+    kurtosis = kurtosis_from(powers, float(all_rows))
+
+    theirs = jnp.dot(rotated, panel_got, preferred_element_type=jnp.float32)
+    mine = jnp.dot(rotated, panel_keep, preferred_element_type=jnp.float32)
+    joined = (mine + swapped(theirs)).astype(jnp.bfloat16)
+
+    write_t, read_t = own_bc(conv_bc, me)
+    taps = jnp.concatenate(
+        [own_cut(conv_x, place, count, 1), own_cut(write_t, place, count, 1), own_cut(read_t, place, count, 1)], 1
+    )
+    kernel = taps.shape[0] - 1
+    seq_len = blks * tok_rows
+    chans = taps.shape[1]
+    padded = jnp.pad(joined[:, :chans].reshape(seqs, seq_len, chans), ((0, 0), (kernel - 1, 0), (0, 0)))
+    conv_sum = taps[kernel]
+    for tap_index in range(kernel):
+        conv_sum = conv_sum + taps[tap_index] * padded[:, tap_index : tap_index + seq_len]
+    convolved = jax.nn.silu(conv_sum).astype(jnp.bfloat16)
+    members = [[g * per_group + i for i in range(per_group)] for g in range(groups_here)]
+    bc = lax.all_gather(
+        convolved[:, :, x_cols:].reshape(all_rows, 2 * bc_cols), ROWS, axis=0, axis_index_groups=members
+    )
+    bc = bc.reshape(per_group, seqs, blks, tok_rows, 2, bc_cols).transpose(4, 1, 2, 3, 0, 5)
+    write, read = bc.reshape(2, seqs, blks, tok_rows, NS)
+    x_heads = convolved[:, :, :x_cols].reshape(seqs, blks, tok_rows, heads, head_size)
+
+    dt = lax.optimization_barrier(joined[:, chans:]).astype(jnp.float32)
+    step = jax.nn.softplus(dt + own_cut(dt_bias, place, count, 0))
+    rate = (step * jnp.exp(own_cut(a_log, place, count, 0))).reshape(seqs, blks, tok_rows, heads)
+    step = step.reshape(seqs, blks, tok_rows, heads)
+    cum = jnp.cumsum(rate, 2)
+    end = cum[:, :, -1]
+    causal = lax.broadcasted_iota(jnp.int32, (tok_rows, tok_rows), 0) >= lax.broadcasted_iota(
+        jnp.int32, (tok_rows, tok_rows), 1
+    )
+    cum_h = cum.transpose(0, 1, 3, 2)
+    spread = cum_h[..., :, None] - cum_h[..., None, :]
+    decay = jnp.where(causal, jnp.exp(-jnp.where(causal, spread, 0.0)), 0.0)
+    scores = jnp.einsum("bktn,bksn->bkts", read, write, preferred_element_type=jnp.float32)
+    weights = (
+        scores[:, :, None] * decay * step.transpose(0, 1, 3, 2)[:, :, :, None, :]
+    ).astype(jnp.bfloat16)
+    within = jnp.einsum("bkhts,bkshp->bkthp", weights, x_heads, preferred_element_type=jnp.float32)
+    update = (
+        (jnp.exp(-(end[:, :, None] - cum)) * step)[..., None] * x_heads.astype(jnp.float32)
+    ).astype(jnp.bfloat16)
+    contrib = jnp.einsum("bkshp,bksn->bkhpn", update, write, preferred_element_type=jnp.float32)
+    state = jnp.zeros_like(contrib[:, 0])
+    states = []
+    for blk in range(blks):
+        states.append(state)
+        state = jnp.exp(-end[:, blk])[..., None, None] * state + contrib[:, blk]
+    carried = jnp.stack(states, 1)
+    read_wide = read.astype(jnp.float32)
+    before = jnp.exp(-cum)[..., None] * jnp.einsum(
+        "bktn,bkhpn->bkthp", read_wide, carried, preferred_element_type=jnp.float32
+    )
+    raw = within + before + own_cut(d_skip, place, count, 0)[:, None] * x_heads.astype(jnp.float32)
+    gain = own_cut(norm_gain, place, count, 0).reshape(heads, head_size)
+    out = (raw * lax.rsqrt(jnp.mean(raw * raw, -1, keepdims=True) + 1e-05) * gain).astype(jnp.bfloat16)
+    out = out.reshape(count, tok_rows, x_cols)
+    out = lax.all_to_all(out, ROWS, 0, 2, tiled=True)
+    return out, kurtosis
+
+
+def shards(tokens, x_weight, bc_weight, dt_weight, *rest):
+    count = lax.axis_size(ROWS)
+    heads_dev = dt_weight.shape[1]
+    groups_here = heads_dev // (HEADS // G)
+    by_heads = (
+        lax.axis_size("mp") == 2
+        and heads_dev % count == 0
+        and groups_here > 0
+        and count % groups_here == 0
+        and tokens.shape[0] == 1
+    )
+    plan = shards_by_heads if by_heads else shards_by_rows
+    return plan(tokens, x_weight, bc_weight, dt_weight, *rest)
+
+
 def solution(mesh):
     return jax.shard_map(
         shards,

time: 583 us -> 302 us (0.52)
  waiting for transfers between devices: 379 us -> 213 us
  blocking collectives: 138 us -> 0 us
  other arithmetic: 12.9 us -> 25.7 us
  matrix products: 30.1 us -> 17.4 us
  starting transfers between devices: 1.66 us -> 13.4 us
  local copies, waits for them, and re-layouts: 6.22 us -> 17.2 us
    all_gather x3 -> x2, waiting for transfers between devices: 377 us -> 96.6 us  [the longest x1 71.2 us: shards_by_heads(): lax.all_gather(rotated_half(tokens[0], me), ROWS, axis=0, tiled=True)]
    all_to_all x0 -> x2, waiting for transfers between devices: none -> 109 us  [the longest x1 92.8 us: shards_by_heads(): panel = lax.all_to_all(pieces, ROWS, 1, 0, tiled=True).reshape(width, -1)]
    psum x1 -> x0, blocking collectives: 74.8 us -> none  [shards(): totals = lax.psum(powers, ('dp', 'ctx'))]
    all_gather x3 -> x0, blocking collectives: 63.2 us -> none  [the longest x1 49.2 us: shards(): lax.all_gather(dt_weight, ('dp', 'ctx'), axis=0, tiled=True)]
    dot_general x9 -> x7, matrix products: 30.1 us -> 17.4 us  [the longest x1 7.85 us: shards_by_heads(): theirs = jnp.dot(rotated, panel_got, preferred_element_type=jnp.float32)]
    all_to_all x0 -> x2, starting transfers between devices: none -> 12.3 us  [the longest x1 7.89 us: shards_by_heads(): panel = lax.all_to_all(pieces, ROWS, 1, 0, tiled=True).reshape(width, -1)]
    reduce_sum x1, other arithmetic: 1.03 us -> 8.68 us  [shards_by_heads(): jnp.sum(square * square, 0)]
    select_n x4 -> x2, other arithmetic: 7.16 us -> 0.1 us  [own_bc(): return (jnp.where(me == 0, keep, got), jnp.where(me == 0, got, keep))]
  transfers between devices with their start and end apart: 4 -> 8, of which waited for: 3 -> 6; matrix products, arithmetic and copies ran while one was open for 3% -> 12% of each run, Pallas kernels for 0% -> 0%
where the time goes in v1:
time: 302 us; the launch traced here: 301 us
  waiting for transfers between devices  213 us (71%)
  other arithmetic  25.7 us (9%)
  matrix products  17.4 us (6%)
  local copies, waits for them, and re-layouts  17.2 us (6%)
  between operations  14.5 us (5%)
  starting transfers between devices  13.4 us (4%)
    all_to_all x1, waiting for transfers between devices, shards_by_heads(): panel = lax.all_to_all(pieces, ROWS, 1, 0, tiled=True).reshape(width, -1)  92.8 us
    all_gather x1, waiting for transfers between devices, shards_by_heads(): lax.all_gather(rotated_half(tokens[0], me), ROWS, axis=0, tiled=True)  71.2 us
    all_gather x1, waiting for transfers between devices, shards_by_heads(): lax.all_gather(convolved[:, :, x_cols:].reshape(all_rows, 2 * bc_cols), R...  25.5 us
    all_to_all x1, waiting for transfers between devices, shards_by_heads(): out = lax.all_to_all(out, ROWS, 0, 2, tiled=True)  16.7 us
    reduce_sum x1, other arithmetic, shards_by_heads(): jnp.sum(square * square, 0)  8.68 us
    all_to_all x1, starting transfers between devices, shards_by_heads(): panel = lax.all_to_all(pieces, ROWS, 1, 0, tiled=True).reshape(width, -1)  7.89 us
    dot_general x1, matrix products, shards_by_heads(): theirs = jnp.dot(rotated, panel_got, preferred_element_type=jnp.float32)  7.85 us
    ppermute x4, waiting for transfers between devices, swapped(): return lax.ppermute(value, 'mp', [(0, 1), (1, 0)])  6.77 us
  transfers between devices with their start and end apart: 8, of which 6 were waited for; matrix products, arithmetic and copies ran while one was open for 12% of the time, Pallas kernels for 0%

profile of v1, /device:TPU:0, one launch (start us, length us, event | category | flops | bytes accessed | tf_op | source)
XLA Modules:
  0.0 301.1 jit_solution(2083011795704902917)
XLA Ops:
  7.2 1.5 copy.83
  12.0 3.3 %copy.47 = bf16[256,4096]{0,1:T(8,128)(2,1)S(1)} copy(bf16[256,4096]{1,0:T(8,128)(2,1)} %param.11) | data formatting | bytes 4194304 | tf_op args[1]
  15.3 1.6 pad_maximum_fusion
  16.9 7.9 %all-to-all-start = ((bf16[256,16,292]{0,2,1:T(8,128)(2,1)}), bf16[256,16,292]{0,2,1:T(8,128)(2,1)S(1)}, u32[]{:S(2)}, u32[]{:S(2)}) async-start(bf16[256,16,292]{0,2,1:T(8,128)(2,1)} %pad_maximum_fusion), calls=%async_computation | async-start | bytes 4849664 | tf_op jit(solution)/shard_map/all_to_all | solution.py:252
  24.8 92.8 %all-to-all-done = bf16[256,16,292]{0,2,1:T(8,128)(2,1)S(1)} async-done(((bf16[256,16,292]{0,2,1:T(8,128)(2,1)}), bf16[256,16,292]{0,2,1:T(8,128)(2,1)S(1)}, u32[]{:S(2)}, u32[]{:S(2)}) %all-to-all-start) | async-done | bytes 2392096 | tf_op jit(solution)/shard_map/all_to_all | solution.py:252
  119.6 3.0 %collective-permute-done.2 = bf16[2048,292]{0,1:T(8,128)(2,1)} collective-permute-done((bf16[2048,292]{0,1:T(8,128)(2,1)S(1)}, bf16[2048,292]{0,1:T(8,128)(2,1)}, u32[]{:S(2)}, u32[]{:S(2)}) %collective-permute-start.2) | collective-permute-done | bytes 1196064 | tf_op jit(solution)/shard_map/ppermute | solution.py:206
  122.6 71.2 %all-gather.3.cloned.1.call-done = bf16[2048,2048]{0,1:T(8,128)(2,1)} async-done(((bf16[128,2048]{0,1:T(8,128)(2,1)}), bf16[2048,2048]{0,1:T(8,128)(2,1)}) %all-gather.3.cloned.1.call-update) | async-done | bytes 8388624 | tf_op jit(solution)/shard_map/all_gather | solution.py:257
  193.8 7.8 %fusion.69 = f32[2048,292]{0,1:T(8,128)} fusion(bf16[2048,2048]{0,1:T(8,128)(2,1)} %all-gather.3.cloned.1.call-done, bf16[2048,292]{0,1:T(8,128)(2,1)} %collective-permute-done.2), kind=kOutput, calls=%fused_computation.123 | convolution fusion | flops 2449473536 | bytes 11976704 | tf_op jit(solution)/shard_map/dot_general | solution.py:268
  202.2 3.7 %collective-permute-done = f32[5,256]{1,0:T(8,128)S(1)} collective-permute-done((f32[5,256]{1,0:T(8,128)S(1)}, f32[5,256]{1,0:T(8,128)S(1)}, u32[]{:S(2)}, u32[]{:S(2)}) %collective-permute-start) | collective-permute-done | bytes 5152 | tf_op jit(solution)/shard_map/ppermute | solution.py:206
  206.1 5.2 %fusion.22 = f32[2048,292]{0,1:T(8,128)S(1)} fusion(bf16[2048,2048]{0,1:T(8,128)(2,1)} %all-gather.3.cloned.1.call-done, bf16[4096,292]{0,1:T(8,128)(2,1)S(1)} %bitcast.83, s32[]{:T(128)S(6)} %select_n.72), kind=kOutput, calls=%fused_computation.37 | convolution fusion | flops 2449473536 | bytes 11993092 | tf_op jit(solution)/shard_map/dot_general | solution.py:269
  211.4 2.0 add_convert_fusion
  213.6 2.0 multiply_convert_fusion.1
  217.8 1.3 copy.64
  219.9 4.9 %reduce_window_sum.11 = f32[4,4,128,4]{3,2,1,0:T(8,128)S(1)} reduce-window(f32[4,4,128,4]{3,2,1,0:T(8,128)S(1)} %bitcast.88, f32[]{:T(128)} %constant.79.clone.1), window={size=1x1x128x1 pad=0_0x0_0x127_0x0_0}, to_apply=%region_0.1 | reduce-window | flops 1040384 | bytes 65540 | tf_op jit(solution)/shard_map/jit(cumsum)/reduce_window_sum | solution.py:296
  225.1 2.5 negate_exponential_fusion
  227.6 1.6 copy.63
  229.5 25.5 %all-gather.5.cloned.1.call-done = bf16[8,2048,32]{1,2,0:T(8,128)(2,1)} async-done(((bf16[1,2048,32]{1,2,0:T(8,128)(2,1)}), bf16[8,2048,32]{1,2,0:T(8,128)(2,1)}) %all-gather.5.cloned.1.call-update) | async-done | bytes 1048592 | tf_op jit(solution)/shard_map/all_gather | solution.py:285
  255.0 1.8 reshape.146
  258.3 1.6 fusion.4
  261.1 1.5 multiply_convert_fusion.3
  262.5 4.4 %all-to-all-start.1 = ((bf16[16,128,256]{1,2,0:T(8,128)(2,1)}), bf16[16,128,256]{1,2,0:T(8,128)(2,1)S(1)}, u32[]{:S(2)}, u32[]{:S(2)}) async-start(bf16[16,128,256]{1,2,0:T(8,128)(2,1)} %bitcast.25), calls=%async_computation.1 | async-start | bytes 2097152 | tf_op jit(solution)/shard_map/all_to_all | solution.py:327
  266.9 8.7 %fusion.2 = (f32[2048]{0:T(1024)S(1)}, f32[2048]{0:T(1024)S(1)}, f32[2048]{0:T(1024)S(1)}, f32[2048]{0:T(1024)S(1)}) fusion(bf16[2048,2048]{0,1:T(8,128)(2,1)} %all-gather.3.cloned.1.call-done), kind=kLoop, calls=%fused_computation.5 | loop fusion | flops 33546240 | bytes 8421376 | tf_op jit(solution)/shard_map/reduce_sum | solution.py:264
  276.2 16.7 %all-to-all-done.1 = bf16[16,128,256]{1,2,0:T(8,128)(2,1)S(1)} async-done(((bf16[16,128,256]{1,2,0:T(8,128)(2,1)}), bf16[16,128,256]{1,2,0:T(8,128)(2,1)S(1)}, u32[]{:S(2)}, u32[]{:S(2)}) %all-to-all-start.1) | async-done | bytes 1048608 | tf_op jit(solution)/shard_map/all_to_all | solution.py:327
  292.9 1.3 copy.79
  (78 shorter events, 12.9 us)
Async XLA Ops:
  7.2 195.0 %copy-start = (f32[5,4096]{1,0:T(8,128)S(1)}, f32[5,4096]{1,0:T(8,128)}, u32[]{:S(2)}) copy-start(f32[5,4096]{1,0:T(8,128)} %param.14) | copy-start | bytes 245764
  7.2 186.6 %all-gather.3.cloned.1.call-start = ((), (), s32[]{:S(2)}) async-start(), calls=%async_computation.2 | async-start | bytes 8912896 | tf_op jit(solution)/shard_map/all_gather | solution.py:257
  10.1 1.0 copy-start.2
  10.1 1.7 copy-start.3
  11.3 3.9 %collective-permute-start.1 = (bf16[256,256]{0,1:T(8,128)(2,1)S(1)}, bf16[256,256]{0,1:T(8,128)(2,1)S(1)}, u32[]{:S(2)}, u32[]{:S(2)}) collective-permute-start(bf16[256,256]{0,1:T(8,128)(2,1)S(1)} %copy.81), channel_id=1, source_target_pairs={{0,1},{1,0},{2,3},{3,2},{4,5},{5,4},{6,7},{7,6},{8,9},{9,8},{10,11... | collective-permute-start | bytes 393224 | tf_op jit(solution)/shard_map/ppermute | solution.py:206
  16.9 100.7 %all-to-all-start = ((bf16[256,16,292]{0,2,1:T(8,128)(2,1)}), bf16[256,16,292]{0,2,1:T(8,128)(2,1)S(1)}, u32[]{:S(2)}, u32[]{:S(2)}) async-start(bf16[256,16,292]{0,2,1:T(8,128)(2,1)} %pad_maximum_fusion), calls=%async_computation | async-start | bytes 4849664 | tf_op jit(solution)/shard_map/all_to_all | solution.py:252
  24.8 230.2 %all-gather.5.cloned.1.call-start = ((), (), s32[]{:S(2)}) async-start(), calls=%async_computation.3 | async-start | bytes 1179648 | tf_op jit(solution)/shard_map/all_gather | solution.py:285
  119.5 82.1 %copy-start.4 = (f32[5,512]{1,0:T(8,128)S(1)}, f32[5,512]{1,0:T(8,128)}, u32[]{:S(2)}) copy-start(f32[5,512]{1,0:T(8,128)} %param.15) | copy-start | bytes 30724
  119.6 3.1 %collective-permute-start.2 = (bf16[2048,292]{0,1:T(8,128)(2,1)S(1)}, bf16[2048,292]{0,1:T(8,128)(2,1)}, u32[]{:S(2)}, u32[]{:S(2)}) collective-permute-start(bf16[2048,292]{0,1:T(8,128)(2,1)S(1)} %constant_dynamic-slice_fusion), channel_id=1, source_target_pairs={{0,1},{1,0},{2,3},{3,2},{4,5},{5,4},{6,7},{7,6},{8,9},{9,8},{10,11... | collective-permute-start | bytes 3588104 | tf_op jit(solution)/shard_map/ppermute | solution.py:206
  201.7 9.7 %collective-permute-start.3 = (f32[2048,292]{0,1:T(8,128)}, f32[2048,292]{0,1:T(8,128)}, u32[]{:S(2)}, u32[]{:S(2)}) collective-permute-start(f32[2048,292]{0,1:T(8,128)} %fusion.69), channel_id=1, source_target_pairs={{0,1},{1,0},{2,3},{3,2},{4,5},{5,4},{6,7},{7,6},{8,9},{9,8},{10,11... | collective-permute-start | bytes 7176200 | tf_op jit(solution)/shard_map/ppermute | solution.py:206
  201.7 4.3 %collective-permute-start = (f32[5,256]{1,0:T(8,128)S(1)}, f32[5,256]{1,0:T(8,128)S(1)}, u32[]{:S(2)}, u32[]{:S(2)}) collective-permute-start(f32[5,256]{1,0:T(8,128)S(1)} %constant_dynamic-slice_fusion.3), channel_id=1, source_target_pairs={{0,1},{1,0},{2,3},{3,2},{4,5},{5,4},{6,7},{7,6},{8,9},{9,8},{10,11... | collective-permute-start | bytes 15368 | tf_op jit(solution)/shard_map/ppermute | solution.py:206
  213.4 3.0 %copy-start.5 = (f32[64]{0:T(128)S(1)}, f32[64]{0:T(128)}, u32[]{:S(2)}) copy-start(f32[64]{0:T(128)} %param.16) | copy-start | bytes 772
  213.4 3.1 %copy-start.6 = (f32[64]{0:T(128)S(1)}, f32[64]{0:T(128)}, u32[]{:S(2)}) copy-start(f32[64]{0:T(128)} %param.18) | copy-start | bytes 772
  213.4 4.0 %copy-start.7 = (f32[64]{0:T(128)S(1)}, f32[64]{0:T(128)}, u32[]{:S(2)}) copy-start(f32[64]{0:T(128)} %param.17) | copy-start | bytes 772
  262.5 30.4 %all-to-all-start.1 = ((bf16[16,128,256]{1,2,0:T(8,128)(2,1)}), bf16[16,128,256]{1,2,0:T(8,128)(2,1)S(1)}, u32[]{:S(2)}, u32[]{:S(2)}) async-start(bf16[16,128,256]{1,2,0:T(8,128)(2,1)} %bitcast.25), calls=%async_computation.1 | async-start | bytes 2097152 | tf_op jit(solution)/shard_map/all_to_all | solution.py:327
  266.9 27.3 %copy-start.1 = (f32[5,4096]{1,0:T(8,128)S(1)}, f32[5,4096]{1,0:T(8,128)}, u32[]{:S(2)}) copy-start(f32[5,4096]{1,0:T(8,128)} %param.14) | copy-start | bytes 245764
Sparse Core Ops, SparseCore 0:
  11.3 182.4 all-gather.2
  216.6 38.3 all-gather.4

commit v2 on v1

--- a/solution.py
+++ b/solution.py
@@ -1,6 +1,8 @@
 import jax
 import jax.numpy as jnp
 from jax import lax
+from jax.experimental import pallas as pl
+from jax.experimental.pallas import tpu as pltpu
 from jax.sharding import PartitionSpec as P
 
 ROOT = 64
@@ -222,6 +224,160 @@
 ROWS = ("dp", "ctx")
 
 
+MESH = pl.DeviceIdType.MESH
+
+
+def greet(peers):
+    barrier = pltpu.get_barrier_semaphore()
+    for peer in peers:
+        pl.semaphore_signal(barrier, inc=1, device_id=peer, device_id_type=MESH)
+    pl.semaphore_wait(barrier, len(peers))
+
+
+def sent(source, target, send_sem, recv_sem, peer):
+    copy = pltpu.make_async_remote_copy(
+        src_ref=source,
+        dst_ref=target,
+        send_sem=send_sem,
+        recv_sem=recv_sem,
+        device_id=peer,
+        device_id_type=MESH,
+    )
+    copy.start()
+    return copy
+
+
+def spread_kernel(
+    rot_ref, piece_ref, all_ref, panel_ref,
+    own_sem, line_send, line_recv, side_send, side_recv, diag_send, diag_recv, part_send, part_recv,
+):
+    dp, ctx, me = lax.axis_index("dp"), lax.axis_index("ctx"), lax.axis_index("mp")
+    blks = lax.axis_size("ctx")
+    count = 4 * blks
+    place = dp * blks + ctx
+    by_x = dp + 1 - 2 * lax.rem(dp, 2)
+    by_y = lax.rem(dp + 2, 4)
+
+    def peer_of(step):
+        other = lax.rem(place + step, count)
+        return other, (other // blks, lax.rem(other, blks), me)
+
+    greet([peer_of(step)[1] for step in range(1, count)])
+    own = [
+        pltpu.make_async_copy(rot_ref, all_ref.at[place], own_sem.at[0]),
+        pltpu.make_async_copy(piece_ref.at[place], panel_ref.at[place], own_sem.at[1]),
+    ]
+    line, side, diag = [], [], []
+
+    def to_sides(step, source, index):
+        for way, corner in ((0, by_x), (1, by_y)):
+            side.append(
+                sent(
+                    source, all_ref.at[index], side_send.at[step, way], side_recv.at[step, way],
+                    (corner, ctx, me),
+                )
+            )
+
+    for step in range(1, blks):
+        to = (dp, lax.rem(ctx + step, blks), me)
+        line.append(
+            sent(rot_ref, all_ref.at[place], line_send.at[step], line_recv.at[step], to)
+        )
+    to_sides(0, rot_ref, place)
+    for copy in own:
+        copy.start()
+    parts = []
+    for step in range(1, count):
+        other, to = peer_of(step)
+        parts.append(
+            sent(
+                piece_ref.at[other], panel_ref.at[place], part_send.at[step], part_recv.at[step], to
+            )
+        )
+
+    half = rot_ref.shape[0] // 2
+    for step in range(blks):
+        source_ctx = lax.rem(ctx - step + blks, blks)
+        if step:
+            line[step - 1].wait_recv()
+            index = dp * blks + source_ctx
+            to_sides(step, all_ref.at[index], index)
+    for step in range(blks):
+        source_ctx = lax.rem(ctx - step + blks, blks)
+        for way, corner, onward in ((0, by_x, by_y), (1, by_y, by_x)):
+            side[2 * step + way].wait_recv()
+            part = all_ref.at[corner * blks + source_ctx, pl.ds(way * half, half)]
+            diag.append(
+                sent(
+                    part, part, diag_send.at[step, way], diag_recv.at[step, way],
+                    (onward, ctx, me),
+                )
+            )
+    for copy in diag + parts:
+        copy.wait_recv()
+    for copy in line + side + diag + parts:
+        copy.wait_send()
+    for copy in own:
+        copy.wait()
+
+
+def exchange_blocks(rotated, pieces, blks):
+    count = 4 * blks
+    dma = pltpu.SemaphoreType.DMA
+    anywhere = pl.BlockSpec(memory_space=pl.ANY)
+    return pl.pallas_call(
+        spread_kernel,
+        out_shape=(
+            jax.ShapeDtypeStruct((count,) + rotated.shape, rotated.dtype),
+            jax.ShapeDtypeStruct(pieces.shape, pieces.dtype),
+        ),
+        in_specs=[anywhere] * 2,
+        out_specs=(anywhere, anywhere),
+        scratch_shapes=[
+            dma((2,)), dma((blks,)), dma((blks,)), dma((blks, 2)), dma((blks, 2)),
+            dma((blks, 2)), dma((blks, 2)), dma((count,)), dma((count,)),
+        ],
+        compiler_params=pltpu.CompilerParams(collective_id=0, has_side_effects=True),
+    )(rotated, pieces)
+
+
+def group_kernel(members, own_ref, all_ref, own_sem, send, recv):
+    dp, ctx, me = lax.axis_index("dp"), lax.axis_index("ctx"), lax.axis_index("mp")
+    blks = lax.axis_size("ctx")
+    place = dp * blks + ctx
+    first = place // members * members
+    seat = place - first
+    peers = []
+    for step in range(1, members):
+        other = first + lax.rem(seat + step, members)
+        peers.append((other // blks, lax.rem(other, blks), me))
+    greet(peers)
+    own = pltpu.make_async_copy(own_ref, all_ref.at[seat], own_sem)
+    own.start()
+    copies = [
+        sent(own_ref, all_ref.at[seat], send.at[step], recv.at[step], peer)
+        for step, peer in enumerate(peers)
+    ]
+    for copy in copies:
+        copy.wait_recv()
+    for copy in copies:
+        copy.wait_send()
+    own.wait()
+
+
+def group_gather(own, members):
+    dma = pltpu.SemaphoreType.DMA
+    anywhere = pl.BlockSpec(memory_space=pl.ANY)
+    return pl.pallas_call(
+        lambda *refs: group_kernel(members, *refs),
+        out_shape=jax.ShapeDtypeStruct((members,) + own.shape, own.dtype),
+        in_specs=[anywhere],
+        out_specs=anywhere,
+        scratch_shapes=[dma, dma((members - 1,)), dma((members - 1,))],
+        compiler_params=pltpu.CompilerParams(collective_id=1, has_side_effects=True),
+    )(own)
+
+
 def shards_by_heads(
     tokens, x_weight, bc_weight, dt_weight, conv_x, conv_bc, dt_bias, a_log, d_skip, norm_gain
 ):
@@ -240,21 +396,36 @@
     head_size = x_cols // heads
 
     write_w, read_w = own_bc(bc_weight, me)
-    pieces = jnp.concatenate(
+    small = jnp.concatenate(
         [
-            x_weight.reshape(depth, count, x_cols),
             write_w.reshape(depth, count, bc_cols),
             read_w.reshape(depth, count, bc_cols),
             dt_weight.reshape(depth, count, heads),
         ],
         2,
     )
-    panel = lax.all_to_all(pieces, ROWS, 1, 0, tiled=True).reshape(width, -1)
+    small_cols = small.shape[2]
+    folds = 4
+    lanes = x_cols // folds
+    small = jnp.pad(small, ((0, 0), (0, 0), (0, lanes - small_cols)))
+    small = small.reshape(folds, depth // folds, count, lanes).transpose(2, 1, 0, 3)
+    pieces = jnp.concatenate(
+        [
+            x_weight.reshape(depth, count, x_cols).transpose(1, 0, 2),
+            small.reshape(count, depth // folds, x_cols),
+        ],
+        1,
+    )
+    rotated, panels = exchange_blocks(rotated_half(tokens[0], me), pieces, blks)
+    rotated = rotated.reshape(all_rows, width // 2)
+    small = panels[:, depth:].reshape(count, depth // folds, folds, lanes).transpose(0, 2, 1, 3)
+    panel = jnp.concatenate(
+        [panels[:, :depth].reshape(width, x_cols), small.reshape(width, lanes)[:, :small_cols]], 1
+    )
     half = width // 2
     panel_keep = lax.dynamic_slice_in_dim(panel, me * half, half, 0)
     panel_got = swapped(lax.dynamic_slice_in_dim(panel, (1 - me) * half, half, 0))
 
-    rotated = lax.all_gather(rotated_half(tokens[0], me), ROWS, axis=0, tiled=True)
     wide = rotated.astype(jnp.float32)
     square = wide * wide
     powers = [
@@ -281,11 +452,9 @@
     for tap_index in range(kernel):
         conv_sum = conv_sum + taps[tap_index] * padded[:, tap_index : tap_index + seq_len]
     convolved = jax.nn.silu(conv_sum).astype(jnp.bfloat16)
-    members = [[g * per_group + i for i in range(per_group)] for g in range(groups_here)]
-    bc = lax.all_gather(
-        convolved[:, :, x_cols:].reshape(all_rows, 2 * bc_cols), ROWS, axis=0, axis_index_groups=members
-    )
-    bc = bc.reshape(per_group, seqs, blks, tok_rows, 2, bc_cols).transpose(4, 1, 2, 3, 0, 5)
+    bc = convolved[:, :, x_cols:].transpose(1, 0, 2).reshape(seq_len, seqs * 2 * bc_cols)
+    bc = group_gather(bc, per_group).reshape(per_group, blks, tok_rows, seqs, 2, bc_cols)
+    bc = bc.transpose(4, 3, 1, 2, 0, 5)
     write, read = bc.reshape(2, seqs, blks, tok_rows, NS)
     x_heads = convolved[:, :, :x_cols].reshape(seqs, blks, tok_rows, heads, head_size)
 
@@ -293,11 +462,11 @@
     step = jax.nn.softplus(dt + own_cut(dt_bias, place, count, 0))
     rate = (step * jnp.exp(own_cut(a_log, place, count, 0))).reshape(seqs, blks, tok_rows, heads)
     step = step.reshape(seqs, blks, tok_rows, heads)
-    cum = jnp.cumsum(rate, 2)
-    end = cum[:, :, -1]
     causal = lax.broadcasted_iota(jnp.int32, (tok_rows, tok_rows), 0) >= lax.broadcasted_iota(
         jnp.int32, (tok_rows, tok_rows), 1
     )
+    cum = jnp.einsum("ts,bksh->bkth", causal.astype(jnp.float32), rate, precision=HIGH)
+    end = cum[:, :, -1]
     cum_h = cum.transpose(0, 1, 3, 2)
     spread = cum_h[..., :, None] - cum_h[..., None, :]
     decay = jnp.where(causal, jnp.exp(-jnp.where(causal, spread, 0.0)), 0.0)
@@ -338,6 +507,7 @@
         and groups_here > 0
         and count % groups_here == 0
         and tokens.shape[0] == 1
+        and lax.axis_size("dp") == 4
     )
     plan = shards_by_heads if by_heads else shards_by_rows
     return plan(tokens, x_weight, bc_weight, dt_weight, *rest)

time: 302 us -> 268 us (0.89)
  waiting for transfers between devices: 213 us -> 25.5 us
  Pallas kernels: 0 us -> 153 us
  local copies, waits for them, and re-layouts: 17.2 us -> 39.6 us
  between operations: 14.5 us -> 1.08 us
  starting transfers between devices: 13.4 us -> 9.28 us
  other arithmetic: 25.7 us -> 21.8 us
    pallas_call x0 -> x2, Pallas kernels: none -> 153 us  [the longest x1 109 us: exchange_blocks(): pl.pallas_call(spread_kernel, out_shape=(jax.ShapeDtypeStruct((count,) +...]
    all_gather x2 -> x0, waiting for transfers between devices: 96.6 us -> none  [the longest x1 71.2 us: shards_by_heads(): lax.all_gather(rotated_half(tokens[0], me), ROWS, axis=0, tiled=True)]
    all_to_all x1 -> x0, waiting for transfers between devices: 92.8 us -> none  [shards_by_heads(): panel = lax.all_to_all(pieces, ROWS, 1, 0, tiled=True).reshape(width, -1)]
    reshape x2 -> x9, local copies, waits for them, and re-layouts: 2.15 us -> 17.7 us  [the longest x2 4.32 us: shards_by_heads(): panels[:, depth:].reshape(count, depth // folds, folds, lanes)]
    all_to_all x1 -> x0, starting transfers between devices: 7.89 us -> none  [shards_by_heads(): panel = lax.all_to_all(pieces, ROWS, 1, 0, tiled=True).reshape(width, -1)]
    slice x2 -> x4, local copies, waits for them, and re-layouts: 0.12 us -> 5.06 us  [the longest x1 3.14 us: shards_by_heads(): panels[:, :depth].reshape(width, x_cols)]
    another operation x1 -> x0, other arithmetic: 4.91 us -> none  [shards_by_heads(): cum = jnp.cumsum(rate, 2)]
    all_to_all x1, starting transfers between devices: 4.37 us -> 8.2 us  [shards_by_heads(): out = lax.all_to_all(out, ROWS, 0, 2, tiled=True)]
  transfers between devices with their start and end apart: 8 -> 5, of which waited for: 6 -> 3; matrix products, arithmetic and copies ran while one was open for 12% -> 11% of each run, Pallas kernels for 0% -> 0%
where the time goes in v2:
time: 268 us; the launch traced here: 267 us
  Pallas kernels  153 us (57%)
  local copies, waits for them, and re-layouts  39.6 us (15%)
  waiting for transfers between devices  25.5 us (10%)
  other arithmetic  21.8 us (8%)
  matrix products  17.4 us (6%)
  starting transfers between devices  9.28 us (3%)
    pallas_call x1, Pallas kernels, exchange_blocks(): pl.pallas_call(spread_kernel, out_shape=(jax.ShapeDtypeStruct((count,) +...  109 us
    pallas_call x1, Pallas kernels, group_gather(): pl.pallas_call(lambda *refs: group_kernel(members, *refs), out_shape=jax....  43.9 us
    all_to_all x1, waiting for transfers between devices, shards_by_heads(): out = lax.all_to_all(out, ROWS, 0, 2, tiled=True)  19.9 us
    all_to_all x1, starting transfers between devices, shards_by_heads(): out = lax.all_to_all(out, ROWS, 0, 2, tiled=True)  8.2 us
    dot_general x1, matrix products, shards_by_heads(): theirs = jnp.dot(rotated, panel_got, preferred_element_type=jnp.float32)  7.63 us
    reduce_sum x1, other arithmetic, shards_by_heads(): jnp.sum(square * square, 0)  6.66 us
    unnamed x24, local copies, waits for them, and re-layouts  5.8 us
    ppermute x4, waiting for transfers between devices, swapped(): return lax.ppermute(value, 'mp', [(0, 1), (1, 0)])  5.62 us
  transfers between devices with their start and end apart: 5, of which 3 were waited for; matrix products, arithmetic and copies ran while one was open for 11% of the time, Pallas kernels for 0%

profile of v2, /device:TPU:0, one launch (start us, length us, event | category | flops | bytes accessed | tf_op | source)
XLA Modules:
  0.0 267.4 jit_solution(8696289004721006524)
XLA Ops:
  9.4 2.1 fusion.33
  12.6 2.5 copy.51
  15.1 2.9 %copy.52 = bf16[256,16,256]{2,0,1:T(8,128)(2,1)S(1)} copy(bf16[256,16,256]{0,2,1:T(8,128)(2,1)} %bitcast.89) | data formatting | bytes 4194304 | tf_op jit(solution)/shard_map/reshape | solution.py:414
  19.7 2.0 reshape.148
  21.8 2.3 copy.55
  24.0 2.1 reshape.149
  26.1 1.8 pad_maximum_fusion.piece_ref
  27.9 108.9 %shard_map.113 = (bf16[16,128,2048]{2,1,0:T(8,128)(2,1)}, bf16[16,320,256]{2,1,0:T(8,128)(2,1)}) custom-call(bf16[128,2048]{1,0:T(8,128)(2,1)} %convert_element_type.65.rot_ref, bf16[16,320,256]{2,1,0:T(8,128)(2,1)} %pad_maximum_fusion.piece_ref), custom_call_target="tpu_custom_call" | custom-call | tf_op jit(solution)/shard_map/pallas_call | solution.py:328
  136.8 1.9 slice.110
  138.7 3.1 %slice.109 = bf16[16,256,256]{2,1,0:T(8,128)(2,1)} slice(bf16[16,320,256]{2,1,0:T(8,128)(2,1)} %get-tuple-element.5), slice={[0:16], [0:256], [0:256]} | slice | bytes 4194304 | tf_op jit(solution)/shard_map/slice | solution.py:423
  141.8 2.9 %copy.57 = bf16[4096,256]{0,1:T(8,128)(2,1)S(1)} copy(bf16[4096,256]{1,0:T(8,128)(2,1)} %bitcast.88) | data formatting | bytes 4194304 | tf_op jit(solution)/shard_map/reshape | solution.py:423
  144.7 2.0 reshape.152
  146.8 2.3 copy.56
  149.1 2.4 reshape.153
  151.8 2.9 %collective-permute-done.2 = bf16[2048,292]{0,1:T(8,128)(2,1)S(1)} collective-permute-done((bf16[2048,292]{0,1:T(8,128)(2,1)S(1)}, bf16[2048,292]{0,1:T(8,128)(2,1)S(1)}, u32[]{:S(2)}, u32[]{:S(2)}) %collective-permute-start.2) | collective-permute-done | bytes 1196064 | tf_op jit(solution)/shard_map/ppermute | solution.py:208
  154.6 7.6 %fusion.79 = f32[2048,292]{0,1:T(8,128)} fusion(bf16[2048,2048]{1,0:T(8,128)(2,1)} %bitcast.85, bf16[2048,292]{0,1:T(8,128)(2,1)S(1)} %collective-permute-done.2), kind=kOutput, calls=%fused_computation.136 | convolution fusion | flops 2449473536 | bytes 11976704 | tf_op jit(solution)/shard_map/dot_general | solution.py:439
  163.9 2.8 %collective-permute-done = f32[5,256]{1,0:T(8,128)S(1)} collective-permute-done((f32[5,256]{1,0:T(8,128)S(1)}, f32[5,256]{1,0:T(8,128)S(1)}, u32[]{:S(2)}, u32[]{:S(2)}) %collective-permute-start) | collective-permute-done | bytes 5152 | tf_op jit(solution)/shard_map/ppermute | solution.py:208
  166.8 5.3 %fusion.24 = f32[2048,292]{0,1:T(8,128)S(1)} fusion(bf16[2048,2048]{1,0:T(8,128)(2,1)} %bitcast.86, s32[]{:T(128)S(6)} %select_n.72, bf16[4096,256]{0,1:T(8,128)(2,1)S(1)} %copy.57, bf16[4096,36]{0,1:T(8,128)(2,1)S(1)} %slice.137), kind=kOutput, calls=%fused_computation.42 | convolution fusion | flops 2451865600 | bytes 13172740 | tf_op jit(solution)/shard_map/dot_general | solution.py:440
  172.2 2.0 add_convert_fusion
  175.3 2.0 multiply_convert_fusion.1
  179.2 43.9 %shard_map.114 = bf16[8,512,128]{2,1,0:T(8,128)(2,1)} custom-call(bf16[512,128]{1,0:T(8,128)(2,1)} %copy.60.refs_0_), custom_call_target="tpu_custom_call" | custom-call | tf_op jit(solution)/shard_map/pallas_call | solution.py:371
  230.7 8.2 %all-to-all-start = ((bf16[16,128,256]{1,2,0:T(8,128)(2,1)}), bf16[16,128,256]{1,2,0:T(8,128)(2,1)S(1)}, u32[]{:S(2)}, u32[]{:S(2)}) async-start(bf16[16,128,256]{1,2,0:T(8,128)(2,1)} %bitcast.31), calls=%async_computation | async-start | bytes 2097152 | tf_op jit(solution)/shard_map/all_to_all | solution.py:496
  238.9 6.7 %fusion.2 = (f32[2048]{0:T(1024)S(1)}, f32[2048]{0:T(1024)S(1)}, f32[2048]{0:T(1024)S(1)}, f32[2048]{0:T(1024)S(1)}) fusion(bf16[16,128,2048]{2,1,0:T(8,128)(2,1)} %get-tuple-element.4), kind=kLoop, calls=%fused_computation.5 | loop fusion | flops 33546240 | bytes 8421376 | tf_op jit(solution)/shard_map/reduce_sum | solution.py:435
  246.2 19.9 %all-to-all-done = bf16[16,128,256]{1,2,0:T(8,128)(2,1)S(1)} async-done(((bf16[16,128,256]{1,2,0:T(8,128)(2,1)}), bf16[16,128,256]{1,2,0:T(8,128)(2,1)S(1)}, u32[]{:S(2)}, u32[]{:S(2)}) %all-to-all-start) | async-done | bytes 1048608 | tf_op jit(solution)/shard_map/all_to_all | solution.py:496
  (84 shorter events, 26.0 us)
Async XLA Ops:
  0.6 162.1 %copy-start = (f32[5,4096]{1,0:T(8,128)S(1)}, f32[5,4096]{1,0:T(8,128)}, u32[]{:S(2)}) copy-start(f32[5,4096]{1,0:T(8,128)} %param.14) | copy-start | bytes 245764
  2.5 15.5 %collective-permute-start.1 = (bf16[256,256]{0,1:T(8,128)(2,1)}, bf16[256,256]{0,1:T(8,128)(2,1)}, u32[]{:S(2)}, u32[]{:S(2)}) collective-permute-start(bf16[256,256]{0,1:T(8,128)(2,1)} %copy.85), channel_id=1, source_target_pairs={{0,1},{1,0},{2,3},{3,2},{4,5},{5,4},{6,7},{7,6},{8,9},{9,8},{10,11... | collective-permute-start | bytes 393224 | tf_op jit(solution)/shard_map/ppermute | solution.py:208
  6.6 2.0 copy-start.5
  7.1 5.5 %copy-start.3 = (bf16[256,4096]{1,0:T(8,128)(2,1)S(1)}, bf16[256,4096]{1,0:T(8,128)(2,1)}, u32[]{:S(2)}) copy-start(bf16[256,4096]{1,0:T(8,128)(2,1)} %param.11) | copy-start | bytes 6291460
  15.1 3.8 %copy-start.4 = (bf16[256,16,4]{0,2,1:T(4,128)(2,1)S(1)}, bf16[256,16,4]{0,2,1:T(4,128)(2,1)}, u32[]{:S(2)}) copy-start(bf16[256,16,4]{0,2,1:T(4,128)(2,1)} %reshape.147) | copy-start | bytes 98308
  151.7 3.0 %collective-permute-start.2 = (bf16[2048,292]{0,1:T(8,128)(2,1)S(1)}, bf16[2048,292]{0,1:T(8,128)(2,1)S(1)}, u32[]{:S(2)}, u32[]{:S(2)}) collective-permute-start(bf16[2048,292]{0,1:T(8,128)(2,1)S(1)} %fusion.22), channel_id=1, source_target_pairs={{0,1},{1,0},{2,3},{3,2},{4,5},{5,4},{6,7},{7,6},{8,9},{9,8},{10,11... | collective-permute-start | bytes 3588104 | tf_op jit(solution)/shard_map/ppermute | solution.py:208
  154.6 7.8 %copy-start.6 = (f32[5,512]{1,0:T(8,128)S(1)}, f32[5,512]{1,0:T(8,128)}, u32[]{:S(2)}) copy-start(f32[5,512]{1,0:T(8,128)} %param.15) | copy-start | bytes 30724
  154.6 8.2 %copy-start.7 = (f32[64]{0:T(128)S(1)}, f32[64]{0:T(128)}, u32[]{:S(2)}) copy-start(f32[64]{0:T(128)} %param.17) | copy-start | bytes 772
  154.6 8.3 %copy-start.8 = (f32[64]{0:T(128)S(1)}, f32[64]{0:T(128)}, u32[]{:S(2)}) copy-start(f32[64]{0:T(128)} %param.16) | copy-start | bytes 772
  154.6 8.3 %copy-start.9 = (f32[64]{0:T(128)S(1)}, f32[64]{0:T(128)}, u32[]{:S(2)}) copy-start(f32[64]{0:T(128)} %param.18) | copy-start | bytes 772
  162.3 9.9 %collective-permute-start.3 = (f32[2048,292]{0,1:T(8,128)}, f32[2048,292]{0,1:T(8,128)}, u32[]{:S(2)}, u32[]{:S(2)}) collective-permute-start(f32[2048,292]{0,1:T(8,128)} %fusion.79), channel_id=1, source_target_pairs={{0,1},{1,0},{2,3},{3,2},{4,5},{5,4},{6,7},{7,6},{8,9},{9,8},{10,11... | collective-permute-start | bytes 7176200 | tf_op jit(solution)/shard_map/ppermute | solution.py:208
  162.4 4.3 %collective-permute-start = (f32[5,256]{1,0:T(8,128)S(1)}, f32[5,256]{1,0:T(8,128)S(1)}, u32[]{:S(2)}, u32[]{:S(2)}) collective-permute-start(f32[5,256]{1,0:T(8,128)S(1)} %constant_dynamic-slice_fusion.2), channel_id=1, source_target_pairs={{0,1},{1,0},{2,3},{3,2},{4,5},{5,4},{6,7},{7,6},{8,9},{9,8},{10,11... | collective-permute-start | bytes 15368 | tf_op jit(solution)/shard_map/ppermute | solution.py:208
  174.2 1.1 copy-start.2
  175.3 2.1 slice-start
  230.7 35.4 %all-to-all-start = ((bf16[16,128,256]{1,2,0:T(8,128)(2,1)}), bf16[16,128,256]{1,2,0:T(8,128)(2,1)S(1)}, u32[]{:S(2)}, u32[]{:S(2)}) async-start(bf16[16,128,256]{1,2,0:T(8,128)(2,1)} %bitcast.31), calls=%async_computation | async-start | bytes 2097152 | tf_op jit(solution)/shard_map/all_to_all | solution.py:496
  238.9 28.5 %copy-start.1 = (f32[5,4096]{1,0:T(8,128)S(1)}, f32[5,4096]{1,0:T(8,128)}, u32[]{:S(2)}) copy-start(f32[5,4096]{1,0:T(8,128)} %param.14) | copy-start | bytes 245764
